TPU v7x, 256 devices: a whole 4x4x8 slice. The times are simulated.
256 devices in a mesh: row: 64 (over z, y, core), col: 4 (over x).
Axes of the slice: x: 4, y: 4, z: 8, core: 2. Of those that a mesh axis runs over, the one named last changes fastest.
Arguments:
- row_embed: float32 [65536, 512], P(('row', 'col')), may hold values from -1.5 to 1.5
- row_accum: float32 [65536, 512], P(('row', 'col')), may hold values from 0.001 to 0.01
- col_embed: float32 [4, 4096, 512], P('col', 'row'), may hold values from -1.5 to 1.5
- col_accum: float32 [4, 4096, 512], P('col', 'row'), may hold values from 0.001 to 0.01
- col_freq: int32 [4, 4096], P('col'), may hold values from 1000 to 29999
- row_freq: int32 [65536], P('row'), may hold values from 1000 to 29999
- block_cols: int32 [64, 4, 2], P('row', 'col'), may hold values from 0 to 3, all different within a row
- counts: int32 [64, 4, 2, 1024, 1024], P('row', 'col'), may hold values from 0 to 1024
- excluded: int32 [512], replicated, may hold values from 0 to 65535
- log_total: float32 [], replicated, may hold values from 15 to 19
Outputs:
- row_embed_new: float32 [65536, 512], P(('row', 'col'))
- row_accum_new: float32 [65536, 512], P(('row', 'col'))
- col_embed_new: float32 [4, 4096, 512], P('col', 'row')
- col_accum_new: float32 [4, 4096, 512], P('col', 'row')
Inputs may be any that keep to these rules, and one draw needn't show every extreme that they name: `block_cols`: the 2 column blocks of one row block and group are different.
All inputs are finite; a program needn't handle non-finite values.
Results may differ from a plain program's by a relative error of at most 0.0071.
The roundings to bfloat16 on the way count: a program that leaves them out, or rounds other values in their place, can miss the bound.
Values may be sent and summed in bfloat16 or wider, within the bound.
A program may use at most 128 MiB of HBM per device.

v0:
```python
import jax
import jax.numpy as jnp
from jax import lax
from jax.sharding import PartitionSpec as P

BLOCK = 1024
learn_rate = 0.2
decay_rate = 0.5


def cell_grads(count_block, predicted, row_logs, col_logs, log_total):
    nonzero = count_block > 0
    safe_count = jnp.where(nonzero, count_block.astype(jnp.float32), jnp.float32(1.0))
    baseline = log_total - row_logs[:, None] - col_logs[None, :]
    weight = 0.1 + 0.25 * jnp.sqrt(safe_count)
    fitted = weight * (predicted - baseline - jnp.log(safe_count))
    hinge_grad = jax.nn.sigmoid(predicted - baseline)
    return (jnp.where(nonzero, fitted, hinge_grad) / BLOCK).astype(jnp.bfloat16)


def body(
    row_embed,
    row_accum,
    col_embed,
    col_accum,
    col_freq,
    row_freq,
    block_cols,
    counts,
    excluded,
    log_total,
):
    block = counts.shape[3]
    slots = counts.shape[2]
    width = row_embed.shape[1]
    own_rows = row_embed.shape[0]
    own_cols = col_embed.shape[1]
    chosen = block_cols[0, 0]
    block_rows = lax.all_gather(row_embed.astype(jnp.bfloat16), "col", axis=0, tiled=True)
    piece = lax.all_gather(col_embed.astype(jnp.bfloat16), "row", axis=1, tiled=True)
    span = piece.shape[1]
    positions = jnp.arange(span, dtype=jnp.int32)
    owner_block = positions // block
    offset = positions - owner_block * block
    target = jnp.full((span,), slots * block, jnp.int32)
    for collect_slot_id in range(slots):
        target = jnp.where(
            owner_block == chosen[collect_slot_id], collect_slot_id * block + offset, target
        )
    fetched = jnp.zeros((slots * block, width), jnp.bfloat16).at[target].set(piece[0], mode="drop")
    row_logs = jnp.log(row_freq.astype(jnp.float32))
    col_logs = jnp.log(col_freq[0].astype(jnp.float32))
    row_grad = jnp.zeros((block, width), jnp.float32)
    col_parts = []
    for slot_id in range(slots):
        col_block = fetched[slot_id * block : (slot_id + 1) * block]
        block_col_logs = lax.dynamic_slice_in_dim(col_logs, chosen[slot_id] * block, block)
        predicted = lax.dot_general(
            block_rows, col_block, (((1,), (1,)), ((), ())), preferred_element_type=jnp.float32
        )
        cell = cell_grads(counts[0, 0, slot_id], predicted, row_logs, block_col_logs, log_total)
        row_grad = row_grad + jnp.dot(cell, col_block, preferred_element_type=jnp.float32)
        col_parts.append(
            lax.dot_general(
                cell, block_rows, (((0,), (0,)), ((), ())), preferred_element_type=jnp.float32
            )
        )
    positions = jnp.arange(own_cols * lax.axis_size("row"), dtype=jnp.int32)
    owner_block = positions // block
    offset = positions - owner_block * block
    summed = jnp.zeros((own_cols * lax.axis_size("row"), width), jnp.float32)
    for slot_id in range(slots):
        picked = jnp.take(col_parts[slot_id], offset, axis=0)
        summed = summed + jnp.where(
            (owner_block == chosen[slot_id])[:, None], picked, jnp.float32(0.0)
        )
    col_grad = lax.psum_scatter(summed, "row", scatter_dimension=0, tiled=True)
    own_grad = lax.psum_scatter(row_grad, "col", scatter_dimension=0, tiled=True)
    col_index = lax.axis_index("col")
    row_index = lax.axis_index("row")
    own_freq = lax.dynamic_slice_in_dim(row_freq, col_index * own_rows, own_rows).astype(
        jnp.float32
    )
    row_ids = row_index * block + col_index * own_rows + jnp.arange(own_rows, dtype=jnp.int32)
    decayed = jnp.all(row_ids[:, None] != excluded[None, :], axis=1)
    freq_root = jnp.sqrt(own_freq)
    decay_coef = jnp.where(decayed, decay_rate * freq_root / (freq_root + 30.0), jnp.float32(0.0))
    full_grad = own_grad + decay_coef[:, None] * row_embed
    row_accum_new = row_accum + full_grad * full_grad
    row_embed_new = row_embed - learn_rate * full_grad / jnp.sqrt(row_accum_new)
    col_step = col_grad[None]
    col_accum_new = col_accum + col_step * col_step
    col_embed_new = col_embed - learn_rate * col_step / jnp.sqrt(col_accum_new)
    return (row_embed_new, row_accum_new, col_embed_new, col_accum_new)


def solution(mesh):
    in_specs = (
        P(("row", "col"), None),
        P(("row", "col"), None),
        P("col", "row", None),
        P("col", "row", None),
        P("col", None),
        P("row"),
        P("row", "col", None),
        P("row", "col", None, None, None),
        P(),
        P(),
    )
    out_specs = (
        P(("row", "col"), None),
        P(("row", "col"), None),
        P("col", "row", None),
        P("col", "row", None),
    )
    return jax.shard_map(body, mesh=mesh, in_specs=in_specs, out_specs=out_specs, check_vma=False)
```

profile of v0, /device:TPU:2, one launch (start us, length us, event | category | flops | bytes accessed | tf_op | source)
XLA Modules:
  0.0 349.1 jit_solution(11396950544478308842)
XLA Ops:
  7.2 1.5 convert_element_type.36
  8.8 1.8 convert_element_type.37
  10.7 1.3 fusion.20
  13.3 8.3 %fusion.19 = (s32[1,1,1,1024,1024]{4,3,2,1,0:T(8,128)}, s32[1,1,1,1024,1024]{4,3,2,1,0:T(8,128)}) fusion(s32[1,1,2,1024,1024]{4,3,2,1,0:T(8,128)} %param.19), kind=kLoop, calls=%fused_computation.56 | loop fusion | bytes 16777216 | tf_op jit(solution)/shard_map/slice | solution.py:61
  21.7 5.4 %copy.20 = s32[1,1,1,1024,1024]{3,4,2,1,0:T(8,128)} copy(s32[1,1,1,1024,1024]{4,3,2,1,0:T(8,128)} %get-tuple-element.10) | data formatting | bytes 8388608
  27.7 5.4 %copy.21 = s32[1,1,1,1024,1024]{3,4,2,1,0:T(8,128)} copy(s32[1,1,1,1024,1024]{4,3,2,1,0:T(8,128)} %get-tuple-element.9) | data formatting | bytes 8388608
  33.2 1.4 compare_select_fusion
  34.5 58.8 %all-gather.3.cloned.1.call-done = bf16[1,4096,512]{2,1,0:T(8,128)(2,1)} async-done(((bf16[1,64,512]{2,1,0:T(8,128)(2,1)}), bf16[1,4096,512]{2,1,0:T(8,128)(2,1)}) %all-gather.3.cloned.1.call-update) | async-done | bytes 4194320 | tf_op jit(solution)/shard_map/all_gather | solution.py:40
  93.4 19.2 %scatter_custom_fusion = bf16[2048,512]{1,0:T(8,128)(2,1)S(1)} fusion(s32[4096]{0:T(1024)S(1)} %bitcast.43, bf16[1,4096,512]{2,1,0:T(8,128)(2,1)} %all-gather.3.cloned.1.call-done, bf16[]{:T(256)} %constant.64.clone.1), kind=kCustom, calls=%fused_computation.9 | custom fusion | bytes 6291458 | tf_op jit(solution)/shard_map/scatter | solution.py:50
  112.6 6.0 %all-gather.5.cloned.1.call-done = bf16[1024,512]{1,0:T(8,128)(2,1)} async-done(((bf16[256,512]{1,0:T(8,128)(2,1)}), bf16[1024,512]{1,0:T(8,128)(2,1)}) %all-gather.5.cloned.1.call-update) | async-done | bytes 1048592 | tf_op jit(solution)/shard_map/all_gather | solution.py:39
  118.6 7.2 %multiply_convert_fusion.1 = bf16[1024,1024]{0,1:T(8,128)(2,1)S(1)} fusion(s32[1,1,1,1024,1024]{3,4,2,1,0:T(8,128)} %copy.20, bf16[1024,512]{1,0:T(8,128)(2,1)} %all-gather.5.cloned.1.call-done, f32[1024]{0:T(1024)S(1)} %bitcast.45, f32[1024]{0:T(1024)S(1)} %log_subtract_fusion, bf16[2048,512]{1,0:T(8,128)(2,1)S(1)} %scatter_custom_fusion), kind=kOutput, calls=%fused_computation.13 | convolution fusion | flops 1089470464 | bytes 8396800 | tf_op jit(solution)/shard_map/dot_general | solution.py:58
  127.2 1.6 copy-done
  129.1 4.1 %multiply_convert_fusion = bf16[1024,1024]{0,1:T(8,128)(2,1)S(1)} fusion(s32[1,1,1,1024,1024]{3,4,2,1,0:T(8,128)S(1)} %copy-done, bf16[1024,512]{1,0:T(8,128)(2,1)S(1)} %copy-done.8, f32[1024]{0:T(1024)S(1)} %bitcast.44, f32[1024]{0:T(1024)S(1)} %log_subtract_fusion, bf16[2048,512]{1,0:T(8,128)(2,1)S(1)} %scatter_custom_fusion), kind=kOutput, calls=%fused_computation.12 | convolution fusion | flops 1089470464 | bytes 8396800 | tf_op jit(solution)/shard_map/dot_general | solution.py:58
  133.3 1.3 copy-done.9
  134.6 2.6 convolution_add_fusion
  137.5 1.3 fusion.12
  138.8 2.8 fusion.22
  141.6 16.8 %gather_fusion.1 = f32[4096,512]{1,0:T(8,128)} fusion(f32[1024,512]{1,0:T(8,128)S(1)} %fusion.22, s32[4096]{0:T(1024)S(1)} %fusion.17), kind=kCustom, calls=%fused_computation.1.clone | custom fusion | bytes 16793600 | tf_op jit(solution)/shard_map/jit(_take)/gather | solution.py:73
  158.4 2.8 fusion.21
  161.3 16.8 %gather_fusion = f32[4096,512]{1,0:T(8,128)} fusion(f32[1024,512]{1,0:T(8,128)S(1)} %fusion.21, s32[4096]{0:T(1024)S(1)} %fusion.17), kind=kCustom, calls=%fused_computation.clone | custom fusion | bytes 16793600 | tf_op jit(solution)/shard_map/jit(_take)/gather | solution.py:73
  178.1 9.9 %fusion = f32[4096,512]{1,0:T(8,128)} fusion(f32[4096,512]{1,0:T(8,128)} %gather_fusion.1, f32[4096,512]{1,0:T(8,128)} %gather_fusion, pred[4096]{0:T(1024)(128)(4,1)S(1)} %compare_and_fusion, pred[4096]{0:T(1024)(128)(4,1)S(1)} %get-tuple-element.15, pred[4096]{0:T(1024)(128)(4,1)S(1)} %get-tuple-element.16), kind=kLoop, calls=%fused_computation.4 | loop fusion | flops 10485760 | bytes 25178112 | tf_op jit(solution)/shard_map/add | solution.py:74
  189.2 2.2 multiply_subtract_fusion
  191.4 149.5 %reduce-scatter.5.cloned.1.call-done = f32[64,512]{1,0:T(8,128)} async-done(((f32[4096,512]{1,0:T(8,128)}), f32[64,512]{1,0:T(8,128)}) %reduce-scatter.5.cloned.1.call-update) | async-done | bytes 131088 | tf_op jit(solution)/shard_map/reduce_scatter | solution.py:77
  340.9 1.6 fusion.9
  (38 shorter events, 3.3 us)
Async XLA Ops:
  7.2 86.2 %all-gather.3.cloned.1.call-start = ((), (), s32[]{:S(2)}) async-start(), calls=%async_computation.2 | async-start | bytes 4259840 | tf_op jit(solution)/shard_map/all_gather | solution.py:40
  8.8 109.9 %all-gather.5.cloned.1.call-start = ((), (), s32[]{:S(2)}) async-start(), calls=%async_computation.3 | async-start | bytes 1310720 | tf_op jit(solution)/shard_map/all_gather | solution.py:39
  10.6 178.3 %reduce-scatter.3.cloned.1.call-start = ((), (), s32[]{:S(2)}) async-start(), calls=%async_computation.4 | async-start | bytes 2621440 | tf_op jit(solution)/shard_map/reduce_scatter | solution.py:78
  27.7 5.4 %copy-start.5 = (s32[1,4096]{1,0:T(1,128)S(1)}, s32[1,4096]{1,0:T(1,128)}, u32[]{:S(2)}) copy-start(s32[1,4096]{1,0:T(1,128)} %param.16) | copy-start | bytes 49156
  27.7 5.4 %copy-start.6 = (s32[1024]{0:T(1024)S(1)}, s32[1024]{0:T(1024)}, u32[]{:S(2)}) copy-start(s32[1024]{0:T(1024)} %param.17) | copy-start | bytes 12292
  125.9 1.3 copy-start.10
  125.9 2.9 copy-start
  125.9 3.2 copy-start.8
  133.3 1.3 copy-start.9
  137.2 203.7 %reduce-scatter.5.cloned.1.call-start = ((), (), s32[]{:S(2)}) async-start(), calls=%async_computation.5 | async-start | bytes 8519680 | tf_op jit(solution)/shard_map/reduce_scatter | solution.py:77
  188.0 0.7 copy-start.7
  188.0 1.1 copy-start.1
  188.0 1.2 copy-start.2
  188.0 152.9 %copy-start.3 = (f32[1,64,512]{2,1,0:T(8,128)S(1)}, f32[1,64,512]{2,1,0:T(8,128)}, u32[]{:S(2)}) copy-start(f32[1,64,512]{2,1,0:T(8,128)} %param.14) | copy-start | bytes 393220
  188.0 152.9 %copy-start.4 = (f32[1,64,512]{2,1,0:T(8,128)S(1)}, f32[1,64,512]{2,1,0:T(8,128)}, u32[]{:S(2)}) copy-start(f32[1,64,512]{2,1,0:T(8,128)} %param.15) | copy-start | bytes 393220
Sparse Core Ops, SparseCore 0:
  11.3 81.9 all-gather.2
  95.7 22.8 all-gather.4
  137.3 32.1 reduce-scatter.2
  188.2 152.6 reduce-scatter.4
where the time goes:
time: 350 us; the launch traced here: 349 us
  waiting for transfers between devices  214 us (61%)
  local copies, waits for them, and re-layouts  77.4 us (22%)
  matrix products  20.9 us (6%)
  other arithmetic  20.1 us (6%)
  between operations  15.9 us (5%)
    reduce_scatter x1, waiting for transfers between devices, body(): col_grad = lax.psum_scatter(summed, 'row', scatter_dimension=0, tiled=True)  149 us
    all_gather x1, waiting for transfers between devices, body(): lax.all_gather(col_embed.astype(jnp.bfloat16), 'row', axis=1, tiled=True)  58.8 us
    gather x2, local copies, waits for them, and re-layouts, body(): picked = jnp.take(col_parts[slot_id], offset, axis=0)  33.6 us
    scatter x1, local copies, waits for them, and re-layouts, body(): jnp.zeros((slots * block, width), jnp.bfloat16).at[target]  19.2 us
    unnamed x24, local copies, waits for them, and re-layouts  14.9 us
    dot_general x2, matrix products, body(): lax.dot_general(block_rows, col_block, (((1,), (1,)), ((), ())), preferre...  11.4 us
    add x1, other arithmetic, body(): summed + jnp.where((owner_block == chosen[slot_id])[:, None], picked, jnp...  9.91 us
    slice x1, local copies, waits for them, and re-layouts, body(): counts[0, 0, slot_id]  8.35 us
  transfers between devices with their start and end apart: 4, of which 3 were waited for; matrix products, arithmetic and copies ran while one was open for 27% of the time, Pallas kernels for 0%

commit v1 on v0

--- a/solution.py
+++ b/solution.py
@@ -37,7 +37,10 @@
     own_cols = col_embed.shape[1]
     chosen = block_cols[0, 0]
     block_rows = lax.all_gather(row_embed.astype(jnp.bfloat16), "col", axis=0, tiled=True)
-    piece = lax.all_gather(col_embed.astype(jnp.bfloat16), "row", axis=1, tiled=True)
+    inner_x = col_embed.astype(jnp.bfloat16)
+    piece = jnp.concatenate(
+        lax.all_to_all(jnp.stack([inner_x] * lax.psum(1, axis_name="row")), "row", 0, 0), axis=1
+    )
     span = piece.shape[1]
     positions = jnp.arange(span, dtype=jnp.int32)
     owner_block = positions // block

time: 350 us -> 365 us (1.043)
  starting transfers between devices: 0.34 us -> 12.6 us
    all_to_all x0 -> x1, waiting for transfers between devices: none -> 72.3 us  [body(): lax.all_to_all(jnp.stack([inner_x] * lax.psum(1, axis_name='row')), 'row'...]
    all_gather x1 -> x0, waiting for transfers between devices: 58.8 us -> none  [body(): lax.all_gather(col_embed.astype(jnp.bfloat16), 'row', axis=1, tiled=True)]
    all_to_all x0 -> x1, starting transfers between devices: none -> 12.5 us  [body(): lax.all_to_all(jnp.stack([inner_x] * lax.psum(1, axis_name='row')), 'row'...]
    all_gather x1, waiting for transfers between devices: 6.05 us -> 0.02 us  [body(): lax.all_gather(row_embed.astype(jnp.bfloat16), 'col', axis=0, tiled=True)]
    reduce_scatter x1, waiting for transfers between devices: 149 us -> 144 us  [body(): col_grad = lax.psum_scatter(summed, 'row', scatter_dimension=0, tiled=True)]
    unnamed x24 -> x26, local copies, waits for them, and re-layouts: 14.9 us -> 14.8 us
  transfers between devices with their start and end apart: 4 -> 4, of which waited for: 3 -> 2; matrix products, arithmetic and copies ran while one was open for 27% -> 26% of each run, Pallas kernels for 0% -> 0%
where the time goes in v1:
time: 365 us
  waiting for transfers between devices  217 us (59%)
  local copies, waits for them, and re-layouts  79.2 us (22%)
  matrix products  21.8 us (6%)
  other arithmetic  18.4 us (5%)
  between operations  15.9 us (4%)
  starting transfers between devices  12.6 us (3%)
    reduce_scatter x1, waiting for transfers between devices, body(): col_grad = lax.psum_scatter(summed, 'row', scatter_dimension=0, tiled=True)  144 us
    all_to_all x1, waiting for transfers between devices, body(): lax.all_to_all(jnp.stack([inner_x] * lax.psum(1, axis_name='row')), 'row'...  72.3 us
    gather x2, local copies, waits for them, and re-layouts, body(): picked = jnp.take(col_parts[slot_id], offset, axis=0)  33.6 us
    scatter x1, local copies, waits for them, and re-layouts, body(): jnp.zeros((slots * block, width), jnp.bfloat16).at[target]  19.4 us
    unnamed x26, local copies, waits for them, and re-layouts  14.8 us
    all_to_all x1, starting transfers between devices, body(): lax.all_to_all(jnp.stack([inner_x] * lax.psum(1, axis_name='row')), 'row'...  12.5 us
    dot_general x2, matrix products, body(): lax.dot_general(block_rows, col_block, (((1,), (1,)), ((), ())), preferre...  11.7 us
    add x1, other arithmetic, body(): summed + jnp.where((owner_block == chosen[slot_id])[:, None], picked, jnp...  9.91 us
  transfers between devices with their start and end apart: 4, of which 2 were waited for; matrix products, arithmetic and copies ran while one was open for 26% of the time, Pallas kernels for 0%

profile of v1, /device:TPU:2, one launch (start us, length us, event | category | flops | bytes accessed | tf_op | source)
XLA Modules:
  0.0 364.7 jit_solution(5300683138511772872)
XLA Ops:
  7.2 0.9 convert_bitcast_fusion
  8.1 2.5 stack.2
  10.6 12.5 %all-to-all-start = ((bf16[64,1,64,512]{3,2,1,0:T(8,128)(2,1)}), bf16[64,1,64,512]{3,2,1,0:T(8,128)(2,1)}, u32[]{:S(2)}, u32[]{:S(2)}) async-start(bf16[64,1,64,512]{3,2,1,0:T(8,128)(2,1)} %stack.2), calls=%async_computation | async-start | bytes 8388608 | tf_op jit(solution)/shard_map/all_to_all | solution.py:42
  25.9 8.3 %fusion.18 = (s32[1,1,1,1024,1024]{4,3,2,1,0:T(8,128)}, s32[1,1,1,1024,1024]{4,3,2,1,0:T(8,128)}) fusion(s32[1,1,2,1024,1024]{4,3,2,1,0:T(8,128)} %param.19), kind=kLoop, calls=%fused_computation.56 | loop fusion | bytes 16777216 | tf_op jit(solution)/shard_map/slice | solution.py:64
  34.2 5.4 %copy.22 = s32[1,1,1,1024,1024]{3,4,2,1,0:T(8,128)} copy(s32[1,1,1,1024,1024]{4,3,2,1,0:T(8,128)} %get-tuple-element.10) | data formatting | bytes 8388608
  40.2 5.4 %copy.23 = s32[1,1,1,1024,1024]{3,4,2,1,0:T(8,128)} copy(s32[1,1,1,1024,1024]{4,3,2,1,0:T(8,128)} %get-tuple-element.9) | data formatting | bytes 8388608
  45.7 1.4 compare_select_fusion
  47.0 72.3 %all-to-all-done = bf16[64,1,64,512]{3,2,1,0:T(8,128)(2,1)} async-done(((bf16[64,1,64,512]{3,2,1,0:T(8,128)(2,1)}), bf16[64,1,64,512]{3,2,1,0:T(8,128)(2,1)}, u32[]{:S(2)}, u32[]{:S(2)}) %all-to-all-start) | async-done | bytes 4194336 | tf_op jit(solution)/shard_map/all_to_all | solution.py:42
  119.3 19.4 %scatter_custom_fusion = bf16[2048,512]{1,0:T(8,128)(2,1)S(1)} fusion(s32[4096]{0:T(1024)S(1)} %bitcast.43, bf16[4096,512]{1,0:T(8,128)(2,1)} %bitcast.6, bf16[]{:T(256)} %constant.64.clone.1), kind=kCustom, calls=%fused_computation.13 | custom fusion | bytes 2097664 | tf_op jit(solution)/shard_map/scatter | solution.py:53
  138.8 7.6 %multiply_convert_fusion.1 = bf16[1024,1024]{0,1:T(8,128)(2,1)S(1)} fusion(s32[1,1,1,1024,1024]{3,4,2,1,0:T(8,128)} %copy.22, bf16[1024,512]{1,0:T(8,128)(2,1)} %all-gather.2.cloned.1.call-done, f32[1024]{0:T(1024)S(1)} %bitcast.45, f32[1024]{0:T(1024)S(1)} %log_subtract_fusion, bf16[2048,512]{1,0:T(8,128)(2,1)S(1)} %scatter_custom_fusion), kind=kOutput, calls=%fused_computation.11 | convolution fusion | flops 1089470464 | bytes 8396800 | tf_op jit(solution)/shard_map/dot_general | solution.py:61
  146.4 1.3 fusion.5
  147.7 1.6 copy-done
  149.6 4.1 %multiply_convert_fusion = bf16[1024,1024]{0,1:T(8,128)(2,1)S(1)} fusion(s32[1,1,1,1024,1024]{3,4,2,1,0:T(8,128)S(1)} %copy-done, bf16[1024,512]{1,0:T(8,128)(2,1)S(1)} %copy-done.9, f32[1024]{0:T(1024)S(1)} %bitcast.44, f32[1024]{0:T(1024)S(1)} %log_subtract_fusion, bf16[2048,512]{1,0:T(8,128)(2,1)S(1)} %scatter_custom_fusion), kind=kOutput, calls=%fused_computation.10 | convolution fusion | flops 1089470464 | bytes 8396800 | tf_op jit(solution)/shard_map/dot_general | solution.py:61
  153.8 1.3 copy-done.10
  155.1 2.6 convolution_add_fusion
  157.8 1.3 fusion.11
  159.1 3.1 fusion.21
  162.2 16.8 %gather_fusion.1 = f32[4096,512]{1,0:T(8,128)} fusion(f32[1024,512]{1,0:T(8,128)S(1)} %fusion.21, s32[4096]{0:T(1024)S(1)} %fusion.16), kind=kCustom, calls=%fused_computation.1.clone | custom fusion | bytes 16793600 | tf_op jit(solution)/shard_map/jit(_take)/gather | solution.py:76
  179.0 3.1 fusion.20
  182.1 16.8 %gather_fusion = f32[4096,512]{1,0:T(8,128)} fusion(f32[1024,512]{1,0:T(8,128)S(1)} %fusion.20, s32[4096]{0:T(1024)S(1)} %fusion.16), kind=kCustom, calls=%fused_computation.clone | custom fusion | bytes 16793600 | tf_op jit(solution)/shard_map/jit(_take)/gather | solution.py:76
  198.9 9.9 %fusion = f32[4096,512]{1,0:T(8,128)} fusion(f32[4096,512]{1,0:T(8,128)} %gather_fusion.1, f32[4096,512]{1,0:T(8,128)} %gather_fusion, pred[4096]{0:T(1024)(128)(4,1)S(1)} %compare_and_fusion, pred[4096]{0:T(1024)(128)(4,1)S(1)} %get-tuple-element.15, pred[4096]{0:T(1024)(128)(4,1)S(1)} %get-tuple-element.16), kind=kLoop, calls=%fused_computation.4 | loop fusion | flops 10485760 | bytes 25178112 | tf_op jit(solution)/shard_map/add | solution.py:77
  209.9 2.2 multiply_subtract_fusion
  212.1 144.5 %reduce-scatter.5.cloned.1.call-done = f32[64,512]{1,0:T(8,128)} async-done(((f32[4096,512]{1,0:T(8,128)}), f32[64,512]{1,0:T(8,128)}) %reduce-scatter.5.cloned.1.call-update) | async-done | bytes 131088 | tf_op jit(solution)/shard_map/reduce_scatter | solution.py:80
  356.6 1.6 fusion.8
  (40 shorter events, 3.0 us)
Async XLA Ops:
  10.6 12.6 %copy-start.1 = (f32[256,512]{1,0:T(8,128)S(1)}, f32[256,512]{1,0:T(8,128)}, u32[]{:S(2)}) copy-start(f32[256,512]{1,0:T(8,128)} %param.12) | copy-start | bytes 1572868
  10.6 13.4 %copy-start.8 = (s32[1,1,2]{2,1,0:T(1,128)S(1)}, s32[1,1,2]{2,1,0:T(1,128)}, u32[]{:S(2)}) copy-start(s32[1,1,2]{2,1,0:T(1,128)} %param.18) | copy-start | bytes 28
  10.6 108.7 %all-to-all-start = ((bf16[64,1,64,512]{3,2,1,0:T(8,128)(2,1)}), bf16[64,1,64,512]{3,2,1,0:T(8,128)(2,1)}, u32[]{:S(2)}, u32[]{:S(2)}) async-start(bf16[64,1,64,512]{3,2,1,0:T(8,128)(2,1)} %stack.2), calls=%async_computation | async-start | bytes 8388608 | tf_op jit(solution)/shard_map/all_to_all | solution.py:42
  23.1 115.7 %all-gather.2.cloned.1.call-start = ((), (), s32[]{:S(2)}) async-start(), calls=%async_computation.3 | async-start | bytes 1310720 | tf_op jit(solution)/shard_map/all_gather | solution.py:39
  23.9 185.9 %reduce-scatter.3.cloned.1.call-start = ((), (), s32[]{:S(2)}) async-start(), calls=%async_computation.4 | async-start | bytes 2621440 | tf_op jit(solution)/shard_map/reduce_scatter | solution.py:81
  40.2 5.4 %copy-start.5 = (s32[1,4096]{1,0:T(1,128)S(1)}, s32[1,4096]{1,0:T(1,128)}, u32[]{:S(2)}) copy-start(s32[1,4096]{1,0:T(1,128)} %param.16) | copy-start | bytes 49156
  40.2 5.5 %copy-start.6 = (s32[1024]{0:T(1024)S(1)}, s32[1024]{0:T(1024)}, u32[]{:S(2)}) copy-start(s32[1024]{0:T(1024)} %param.17) | copy-start | bytes 12292
  146.4 1.4 copy-start.11
  146.4 2.9 copy-start
  146.4 3.2 copy-start.9
  153.7 1.3 copy-start.10
  157.7 198.9 %reduce-scatter.5.cloned.1.call-start = ((), (), s32[]{:S(2)}) async-start(), calls=%async_computation.5 | async-start | bytes 8519680 | tf_op jit(solution)/shard_map/reduce_scatter | solution.py:80
  208.8 0.7 copy-start.7
  208.8 1.1 copy-start.2
  208.8 147.8 %copy-start.3 = (f32[1,64,512]{2,1,0:T(8,128)S(1)}, f32[1,64,512]{2,1,0:T(8,128)}, u32[]{:S(2)}) copy-start(f32[1,64,512]{2,1,0:T(8,128)} %param.14) | copy-start | bytes 393220
  208.8 147.7 %copy-start.4 = (f32[1,64,512]{2,1,0:T(8,128)S(1)}, f32[1,64,512]{2,1,0:T(8,128)}, u32[]{:S(2)}) copy-start(f32[1,64,512]{2,1,0:T(8,128)} %param.15) | copy-start | bytes 393220
Sparse Core Ops, SparseCore 0:
  26.3 26.3 all-gather.1
  157.8 27.0 reduce-scatter.2
  209.0 147.5 reduce-scatter.4
